TPU v7x, 128 devices: a whole 4x4x4 slice. The times are simulated.
128 devices in a mesh: row: 16 (over y, x), col: 8 (over z, core).
Axes of the slice: x: 4, y: 4, z: 4, core: 2. Of those that a mesh axis runs over, the one named last changes fastest.
Arguments:
- occ_coef: bfloat16 [1024, 16384], P('row', 'col'), may hold values from -6 to 6
- vir_coef: bfloat16 [2048, 16384], P('row', 'col'), may hold values from -6 to 6
- atom_counts: int32 [8, 768], P('col'), may hold values from 1 to 9, 2048 in all within a row
- occ_index: int32 [1024], P('row'), may hold values from 0 to 1023
- vir_index: int32 [1024], P('row'), may hold values from 0 to 2047
- interaction: bfloat16 [6144, 6144], P('col', 'row'), as said below
- window_charges: bfloat16 [131072, 6144], P(('row', 'col')), may hold values from -0.078125 to 0.078125
- panel_start: int32 [1], replicated, may hold values from 0 to 130048
Outputs:
- coupling: bfloat16 [1024, 131072], P(None, ('row', 'col'))
Inputs may be any that keep to these rules, and one draw needn't show every extreme that they name: Each line of atom_counts sums to 2048. interaction is symmetric, with its diagonal between 0.5 and 1.5.
All inputs are finite; a program needn't handle non-finite values.
Results may differ from a plain program's by a relative error of at most 0.017.
Values may be sent and summed in bfloat16 or wider, within the bound.
A program may use at most 128 MiB of HBM per device.

v0:
```python
import jax
import jax.numpy as jnp
from jax import lax
from jax.sharding import PartitionSpec as P


def fold_rows(window_charges):

    def add_rows(running, block_in, first_row):
        return lax.dot_general(
            block_in, window_charges, (((0,), (1,)), ((), ())), preferred_element_type=jnp.float32
        )

    return add_rows


def shards(
    occ_coef, vir_coef, atom_counts, occ_index, vir_index, interaction, window_charges, panel_start
):
    occ_all, vir_all = (
        lax.all_gather(occ_coef, "row", axis=0, tiled=True),
        lax.all_gather(vir_coef, "row", axis=0, tiled=True),
    )
    counts = atom_counts[0]
    atom_ends = jnp.cumsum(counts, dtype=jnp.int32)
    atom_starts = atom_ends - counts
    basis_index = lax.broadcasted_iota(jnp.int32, (occ_all.shape[1], counts.shape[0]), 0)
    member = jnp.logical_and(
        basis_index >= atom_starts[None, :], basis_index < atom_ends[None, :]
    ).astype(jnp.bfloat16)
    density = jnp.take(occ_all, occ_index, axis=0).astype(jnp.float32) * jnp.take(
        vir_all, vir_index, axis=0
    ).astype(jnp.float32)
    upper_part = density.astype(jnp.bfloat16)
    lower_part = (density - upper_part.astype(jnp.float32)).astype(jnp.bfloat16)
    summed_upper = jnp.dot(upper_part, member, preferred_element_type=jnp.float32)
    summed_lower = jnp.dot(lower_part, member, preferred_element_type=jnp.float32)
    panel_charges = lax.all_gather(
        (summed_upper + summed_lower).astype(jnp.bfloat16), "row", axis=0, tiled=True
    )
    win_rows = window_charges.shape[0]
    empty_sum = jnp.zeros((panel_charges.shape[0], win_rows), jnp.float32)
    add_rows = fold_rows(window_charges)
    partial_value = lax.dot_general(
        interaction, panel_charges, (((0,), (1,)), ((), ())), preferred_element_type=jnp.float32
    )
    summed = lax.psum(partial_value, "col")
    coupling = add_rows(
        empty_sum,
        lax.all_gather(summed.astype(jnp.bfloat16), "row", axis=0, tiled=True),
        jnp.int32(0),
    )
    panel_index = lax.broadcasted_iota(jnp.int32, coupling.shape, 0)
    window_index = lax.axis_index(("row", "col")) * win_rows + lax.broadcasted_iota(
        jnp.int32, coupling.shape, 1
    )
    upper_mask = window_index >= panel_start[0] + panel_index
    return jnp.where(upper_mask, coupling, jnp.zeros_like(coupling)).astype(jnp.bfloat16)


def solution(mesh):
    placed = (
        P("row", "col"),
        P("row", "col"),
        P("col", None),
        P("row"),
        P("row"),
        P("col", "row"),
        P(("row", "col"), None),
        P(),
    )
    return jax.shard_map(
        shards, mesh=mesh, in_specs=placed, out_specs=P(None, ("row", "col")), check_vma=False
    )
```

profile of v0, /device:TPU:1, one launch (start us, length us, event | category | flops | bytes accessed | tf_op | source)
XLA Modules:
  0.0 369.2 jit_solution(8494702006687040566)
XLA Ops:
  6.5 0.7 all-gather.5.cloned.1.call-update
  7.3 0.7 all-gather.7.cloned.1.call-update
  8.0 0.0 all-gather.9.cloned.1.call-start
  8.1 0.7 reduce
  8.8 0.3 reduce-window.9
  9.0 0.1 slice.7
  9.1 0.7 compare_select_fusion
  9.8 0.7 compare_select_fusion.1
  10.5 0.1 slice_reduce_fusion
  10.6 0.1 add_bitcast_fusion.1
  10.7 0.7 fusion.17
  11.4 0.7 compare_and_fusion
  12.0 52.1 %all-gather.5.cloned.1.call-done = bf16[1024,2048]{1,0:T(8,128)(2,1)} async-done(((bf16[64,2048]{1,0:T(8,128)(2,1)}), bf16[1024,2048]{1,0:T(8,128)(2,1)}) %all-gather.5.cloned.1.call-update) | async-done | bytes 4194320 | tf_op jit(solution)/shard_map/all_gather | solution.py:21
  64.1 3.7 %gather_fusion = bf16[64,2048]{1,0:T(8,128)(2,1)S(1)} fusion(bf16[1024,2048]{1,0:T(8,128)(2,1)} %all-gather.5.cloned.1.call-done, s32[1024]{0:T(1024)S(1)} %pad_clamp_fusion.1), kind=kCustom, calls=%fused_computation | custom fusion | bytes 524544 | tf_op jit(solution)/shard_map/jit(_take)/gather | solution.py:31
  67.9 68.8 %all-gather.7.cloned.1.call-done = bf16[2048,2048]{1,0:T(8,128)(2,1)} async-done(((bf16[128,2048]{1,0:T(8,128)(2,1)}), bf16[2048,2048]{1,0:T(8,128)(2,1)}) %all-gather.7.cloned.1.call-update) | async-done | bytes 8388624 | tf_op jit(solution)/shard_map/all_gather | solution.py:22
  136.6 5.4 %gather_fusion.1 = bf16[64,2048]{1,0:T(8,128)(2,1)S(1)} fusion(bf16[2048,2048]{1,0:T(8,128)(2,1)} %all-gather.7.cloned.1.call-done, s32[1024]{0:T(1024)S(1)} %pad_clamp_fusion), kind=kCustom, calls=%fused_computation.1 | custom fusion | bytes 524544 | tf_op jit(solution)/shard_map/jit(_take)/gather | solution.py:31
  142.1 2.0 fusion.1
  144.1 2.6 fusion.12
  146.7 0.0 all-gather.11.cloned.1.call-start
  146.7 42.7 %all-gather.9.cloned.1.call-done = bf16[1024,768]{1,0:T(8,128)(2,1)} async-done(((bf16[64,768]{1,0:T(8,128)(2,1)}), bf16[1024,768]{1,0:T(8,128)(2,1)}) %all-gather.9.cloned.1.call-update) | async-done | bytes 1572880 | tf_op jit(solution)/shard_map/all_gather | solution.py:38
  189.4 2.4 convolution_bitcast_fusion
  191.8 52.0 %all-reduce.1 = bf16[384,1024]{0,1:T(8,128)(2,1)} all-reduce(f32[384,1024]{0,1:T(8,128)S(1)} %convolution_bitcast_fusion), channel_id=1, replica_groups=mesh['row'=16,'col'=8] {'col'}, use_global_device_ids=true, to_apply=%region_2.3 | all-reduce | flops 393216 | bytes 2359296 | tf_op jit(solution)/shard_map/psum | solution.py:47
  244.5 98.0 %all-gather.11.cloned.1.call-done = bf16[6144,1024]{0,1:T(8,128)(2,1)} async-done(((bf16[384,1024]{0,1:T(8,128)(2,1)}), bf16[6144,1024]{0,1:T(8,128)(2,1)}) %all-gather.11.cloned.1.call-update) | async-done | bytes 12582928 | tf_op jit(solution)/shard_map/all_gather | solution.py:50
  342.4 20.2 %select_convert_fusion = bf16[1024,1024]{1,0:T(8,128)(2,1)} fusion(bf16[6144,1024]{0,1:T(8,128)(2,1)} %all-gather.11.cloned.1.call-done, bf16[1024,6144]{1,0:T(8,128)(2,1)} %param.14, s32[1024]{0:T(1024)S(1)} %get-tuple-element.10, s32[1024]{0:T(1024)S(1)} %get-tuple-element.9), kind=kOutput, calls=%fused_computation.7 | convolution fusion | flops 12888047616 | bytes 27271168 | tf_op jit(solution)/shard_map/dot_general | solution.py:10
  (10 shorter events, 0.1 us)
Async XLA Ops:
  6.5 182.9 %copy-start = (bf16[768,384]{1,0:T(8,128)(2,1)S(1)}, bf16[768,384]{1,0:T(8,128)(2,1)}, u32[]{:S(2)}) copy-start(bf16[768,384]{1,0:T(8,128)(2,1)} %param.13) | copy-start | bytes 1769476
  6.5 57.6 %all-gather.5.cloned.1.call-start = ((), (), s32[]{:S(2)}) async-start(), calls=%async_computation | async-start | bytes 4456448 | tf_op jit(solution)/shard_map/all_gather | solution.py:21
  7.3 129.4 %all-gather.7.cloned.1.call-start = ((), (), s32[]{:S(2)}) async-start(), calls=%async_computation.1 | async-start | bytes 8912896 | tf_op jit(solution)/shard_map/all_gather | solution.py:22
  8.0 181.4 %all-gather.9.cloned.1.call-start = ((), (), s32[]{:S(2)}) async-start(), calls=%async_computation.2 | async-start | bytes 1671168 | tf_op jit(solution)/shard_map/all_gather | solution.py:38
  146.7 195.8 %all-gather.11.cloned.1.call-start = ((), (), s32[]{:S(2)}) async-start(), calls=%async_computation.3 | async-start | bytes 13369344 | tf_op jit(solution)/shard_map/all_gather | solution.py:50
Sparse Core Ops, SparseCore 0:
  9.5 54.5 all-gather.4
  66.3 70.3 all-gather.6
  146.8 42.5 all-gather.8
  243.9 98.4 all-gather.10
where the time goes:
time: 370 us; the launch traced here: 369 us
  waiting for transfers between devices  263 us (71%)
  blocking collectives  52 us (14%)
  matrix products  27.1 us (7%)
  between operations  13.8 us (4%)
  local copies, waits for them, and re-layouts  9.35 us (3%)
  other arithmetic  3.79 us (1%)
    all_gather x1, waiting for transfers between devices, shards(): lax.all_gather(summed.astype(jnp.bfloat16), 'row', axis=0, tiled=True)  98 us
    all_gather x1, waiting for transfers between devices, shards(): lax.all_gather(vir_coef, 'row', axis=0, tiled=True)  68.8 us
    all_gather x1, waiting for transfers between devices, shards(): lax.all_gather(occ_coef, 'row', axis=0, tiled=True)  52.1 us
    psum x1, blocking collectives, shards(): summed = lax.psum(partial_value, 'col')  52 us
    all_gather x1, waiting for transfers between devices, shards(): lax.all_gather((summed_upper + summed_lower).astype(jnp.bfloat16), 'row',...  42.7 us
    dot_general x1, matrix products, add_rows(): lax.dot_general(block_in, window_charges, (((0,), (1,)), ((), ())), prefe...  20.2 us
  transfers between devices with their start and end apart: 4, of which 4 were waited for; matrix products, arithmetic and copies ran while one was open for 2% of the time, Pallas kernels for 0%

commit v1 on v0

v1 whole, which is shorter than its diff:
```python
import jax
import jax.numpy as jnp
from jax import lax
from jax.experimental import pallas as pl
from jax.experimental.pallas import tpu as pltpu
from jax.sharding import PartitionSpec as P

MESH = pl.DeviceIdType.MESH
BF = jnp.bfloat16
F32 = jnp.float32


def place():
    row, col = lax.axis_index("row"), lax.axis_index("col")
    return lax.div(row, 4), lax.rem(row, 4), lax.div(col, 2), lax.rem(col, 2)


def step(c, d):
    return lax.rem(c + d, 4)


def device(y, x, z, k):
    return (y * 4 + x, z * 2 + k)


def send(src, dst, send_sem, recv_sem, target):
    copy = pltpu.make_async_remote_copy(
        src_ref=src, dst_ref=dst, send_sem=send_sem, recv_sem=recv_sem, device_id=target, device_id_type=MESH
    )
    copy.start()
    return copy


def arrived(ref, send_sem, recv_sem, me):
    pltpu.make_async_remote_copy(
        src_ref=ref, dst_ref=ref, send_sem=send_sem, recv_sem=recv_sem, device_id=me, device_id_type=MESH
    ).wait_recv()


def greet(targets):
    barrier = pltpu.get_barrier_semaphore()
    for target in targets:
        pl.semaphore_signal(barrier, inc=1, device_id=target, device_id_type=MESH)
    pl.semaphore_wait(barrier, len(targets))


def iota(shape, dim):
    return lax.broadcasted_iota(jnp.int32, shape, dim).astype(F32)


def front(idx_hbm, occ_hbm, vir_hbm, counts_ref, inter_hbm, out_ref,
          idx_all, occ_t, vir_t, pick_occ, pick_vir, member, dens_out, dens, charges, inter, half_out, half_in,
          quarter_out, quarter_in,
          idx_s, idx_r, occ_s, occ_r, vir_s, vir_r, dens_s, dens_r, ag_s, ag_r, rs_s, rs_r, loc):
    y, x, z, k = place()
    me = device(y, x, z, k)
    r = y * 4 + x
    plane = [(step(y, d // 4), step(x, d % 4)) for d in range(1, 16)]
    greet(
        [device(yy, xx, z, k) for yy, xx in plane]
        + [device(y, x, step(z, d), k) for d in (1, 2, 3)]
        + [device(y, x, z, 1 - k)]
    )
    sent = []
    own = [
        pltpu.make_async_copy(idx_hbm, idx_all.at[r], idx_r.at[r]),
        pltpu.make_async_copy(occ_hbm.at[:, pl.ds(pl.multiple_of(r * 128, 128), 128)], occ_t.at[r], occ_r.at[r]),
        pltpu.make_async_copy(vir_hbm.at[:, pl.ds(pl.multiple_of(r * 128, 128), 128)], vir_t.at[r], vir_r.at[r]),
        pltpu.make_async_copy(inter_hbm, inter, loc.at[0]),
    ]
    for copy in own:
        copy.start()
    for d, (yy, xx) in enumerate(plane):
        sent.append(send(idx_hbm, idx_all.at[r], idx_s.at[d], idx_r.at[r], device(yy, xx, z, k)))
    for d, (yy, xx) in enumerate(plane):
        cols = pl.ds(pl.multiple_of((yy * 4 + xx) * 128, 128), 128)
        sent.append(send(occ_hbm.at[:, cols], occ_t.at[r], occ_s.at[d], occ_r.at[r], device(yy, xx, z, k)))
    for d, (yy, xx) in enumerate(plane):
        cols = pl.ds(pl.multiple_of((yy * 4 + xx) * 128, 128), 128)
        sent.append(send(vir_hbm.at[:, cols], vir_t.at[r], vir_s.at[d], vir_r.at[r], device(yy, xx, z, k)))
    counts = counts_ref[...].astype(F32)
    upper = (iota((768, 768), 0) <= iota((768, 768), 1)).astype(BF)
    ends = jnp.dot(jnp.broadcast_to(counts, (8, 768)).astype(BF), upper, preferred_element_type=F32)[0:1]
    starts = ends - counts

    def members(i, carry):
        basis = iota((256, 768), 0) + (i * 256).astype(F32)
        inside = jnp.logical_and(basis >= starts, basis < ends)
        member[pl.ds(pl.multiple_of(i * 256, 256), 256), :] = jnp.where(inside, 1.0, 0.0).astype(BF)
        return carry

    lax.fori_loop(0, 8, members, 0)

    for s in range(16):
        arrived(idx_all.at[s], idx_s.at[0], idx_r.at[s], me)

    def picks(s, carry):
        line = idx_all[s][0:1].astype(F32)
        mine = iota((128, 128), 0) == iota((128, 128), 1)
        column = jnp.sum(jnp.where(mine, jnp.broadcast_to(line, (128, 128)), 0.0), axis=1, keepdims=True)
        rows = pl.ds(pl.multiple_of(s * 64, 64), 64)
        pick_occ[rows, :] = jnp.where(column[0:64] == iota((64, 1024), 1), 1.0, 0.0).astype(BF)
        pick_vir[rows, :] = jnp.where(column[64:128] == iota((64, 2048), 1), 1.0, 0.0).astype(BF)
        return carry

    lax.fori_loop(0, 16, picks, 0)
    for s in range(16):
        arrived(occ_t.at[s], occ_s.at[0], occ_r.at[s], me)
    for s in range(16):
        arrived(vir_t.at[s], vir_s.at[0], vir_r.at[s], me)
    occ_rows, vir_rows = occ_t[...].reshape(1024, 128), vir_t[...].reshape(2048, 128)
    n = 0
    for dy in (1, 2, 3, 0):
        yy = step(y, dy)
        rows = pl.ds(pl.multiple_of(yy * 256, 256), 256)
        first = jnp.dot(pick_occ[rows, :], occ_rows, preferred_element_type=F32)
        second = jnp.dot(pick_vir[rows, :], vir_rows, preferred_element_type=F32)
        dens_out[pl.ds(yy * 4, 4)] = (first * second).astype(BF).reshape(4, 64, 128)
        for dx in (1, 2, 3, 0):
            xx = step(x, dx)
            other = yy * 4 + xx
            if dy == 0 and dx == 0:
                pltpu.make_async_copy(dens_out.at[r], dens.at[r], dens_r.at[r]).start()
            else:
                sent.append(send(dens_out.at[other], dens.at[r], dens_s.at[n], dens_r.at[r], device(yy, xx, z, k)))
                n += 1
    for s in range(16):
        arrived(dens.at[s], dens_s.at[0], dens_r.at[s], me)
    density = jnp.concatenate([dens[s] for s in range(16)], axis=1)
    charges[y, x] = jnp.dot(density, member[...], preferred_element_type=F32).astype(BF)
    n = [0]

    def slot():
        n[0] += 1
        return ag_s.at[n[0] - 1], ag_r.at[n[0] - 1]

    a_up, a_down = device(y, step(x, 1), z, k), device(y, step(x, 3), z, k)
    b_up, b_down = device(step(y, 1), x, z, k), device(step(y, 3), x, z, k)

    def stage(parts):
        slots = []
        for whole, half, c, up, down in parts:
            four = [slot() for _ in range(4)]
            slots.append(four)
            sent.append(send(whole(c), whole(c), *four[0], up))
            sent.append(send(whole(c), whole(c), *four[1], down))
        for (whole, half, c, up, down), four in zip(parts, slots):
            arrived(whole(step(c, 3)), *four[0], me)
            sent.append(send(half(step(c, 3), 0), half(step(c, 3), 0), *four[2], up))
            arrived(whole(step(c, 1)), *four[1], me)
            sent.append(send(half(step(c, 1), 1), half(step(c, 1), 1), *four[3], down))
        for (whole, half, c, up, down), four in zip(parts, slots):
            arrived(half(step(c, 2), 0), *four[2], me)
            arrived(half(step(c, 2), 1), *four[3], me)

    stage([
        (lambda s: charges.at[y, s, pl.ds(0, 32)], lambda s, h: charges.at[y, s, pl.ds(16 * h, 16)], x, a_up, a_down),
        (lambda s: charges.at[s, x, pl.ds(32, 32)], lambda s, h: charges.at[s, x, pl.ds(32 + 16 * h, 16)], y, b_up, b_down),
    ])
    stage([
        (lambda s: charges.at[s, :, pl.ds(0, 32)], lambda s, h: charges.at[s, pl.ds(2 * h, 2), pl.ds(0, 32)], y, b_up, b_down),
        (lambda s: charges.at[:, s, pl.ds(32, 32)], lambda s, h: charges.at[pl.ds(2 * h, 2), s, pl.ds(32, 32)], x, a_up, a_down),
    ])
    own[3].wait()
    theirs = charges[pl.ds((1 - k) * 2, 2)].reshape(512, 768)
    half_out[...] = jnp.dot(theirs, inter[...], preferred_element_type=F32)
    swap = send(half_out, half_in, rs_s.at[0], rs_r.at[0], device(y, x, z, 1 - k))
    sent.append(swap)
    mine = jnp.dot(charges[pl.ds(k * 2, 2)].reshape(512, 768), inter[...], preferred_element_type=F32)
    swap.wait_recv()
    quarter_out[...] = (mine + half_in[...]).reshape(4, 128, 384)
    for d in (1, 2, 3):
        zz = step(z, d)
        quarter_in[d, 0] = quarter_out[zz].astype(BF)
        sent.append(send(quarter_in.at[d, 0], quarter_in.at[d, 1], rs_s.at[d], rs_r.at[d], device(y, x, zz, k)))
    total = quarter_out[z]
    for d in (1, 2, 3):
        arrived(quarter_in.at[d, 1], rs_s.at[d], rs_r.at[d], me)
        total = total + quarter_in[d, 1].astype(F32)
    total = total.astype(BF)
    for j in range(3):
        out_ref[j] = total[:, 128 * j:128 * j + 128]
    for copy in sent:
        copy.wait_send()


def back(block_ref, win_hbm, out_ref, pot, win, acc, ici_s, ici_r, d2d_s, d2d_r, loc):
    y, x, z, k = place()
    me = device(y, x, z, k)

    def load(i, carry):
        cols = pl.ds(pl.multiple_of(i * 128, 128), 128)
        pltpu.make_async_copy(win_hbm.at[:, cols], win.at[i], loc.at[0]).start()
        return carry

    lax.fori_loop(0, 48, load, 0)
    ups = {"y": device(step(y, 1), x, z, k), "x": device(y, step(x, 1), z, k), "z": device(y, x, step(z, 1), k)}
    downs = {"y": device(step(y, 3), x, z, k), "x": device(y, step(x, 3), z, k), "z": device(y, x, step(z, 3), k)}
    at = {"y": y, "x": x, "z": z}
    twin = device(y, x, z, 1 - k)
    greet(list(ups.values()) + list(downs.values()) + [twin])
    sent = []

    def rows(s, kk=k, n=128, h=0):
        return pl.ds(pl.multiple_of(kk * 512 + s * 128 + h, 64), n)

    def half_rows(kk=k):
        return pl.ds(pl.multiple_of(kk * 512, 512), 512)

    mine = rows(z)
    orders = ("zyx", "xzy", "yxz")
    first = (
        lambda s, h=None: pot.at[0, y, x, rows(s) if h is None else rows(s, n=64, h=64 * h)],
        lambda s, h=None: pot.at[1, y, s, mine if h is None else rows(z, n=64, h=64 * h)],
        lambda s, h=None: pot.at[2, s, x, mine if h is None else rows(z, n=64, h=64 * h)],
    )
    second = (
        lambda s, h=None, kk=k: pot.at[0, s, x, half_rows(kk) if h is None else pl.ds(pl.multiple_of(kk * 512 + 256 * h, 256), 256)],
        lambda s, h=None, kk=k: pot.at[1, y, slice(None) if h is None else pl.ds(2 * h, 2), rows(s, kk)],
        lambda s, h=None, kk=k: pot.at[2, slice(None) if h is None else pl.ds(2 * h, 2), s, rows(z, kk)],
    )
    third = (
        lambda s, q, kk=k: pot.at[0, q, s, half_rows(kk)],
        lambda s, q, kk=k: pot.at[1, s, q, half_rows(kk)],
        lambda s, q, kk=k: pot.at[2, q, :, rows(s, kk)],
    )
    for j in range(3):
        pot[j, y, x, mine, :] = block_ref[j]

    n_ici, n_d2d = [0, 0, 0], [0, 0, 0]

    def slot(j):
        n_ici[j] += 1
        return ici_s.at[j, n_ici[j] - 1], ici_r.at[j, n_ici[j] - 1]

    def share(j, ref):
        n_d2d[j] += 1
        sems = d2d_s.at[j, n_d2d[j] - 1], d2d_r.at[j, n_d2d[j] - 1]
        sent.append(send(ref, ref, *sems, twin))
        return sems

    def ring(level, views):
        slots = []
        for j in range(3):
            c, axis = at[orders[j][level]], orders[j][level]
            four = [slot(j) for _ in range(4)]
            slots.append(four)
            sent.append(send(views[j](c), views[j](c), *four[0], ups[axis]))
            sent.append(send(views[j](c), views[j](c), *four[1], downs[axis]))
        for j in range(3):
            c, axis = at[orders[j][level]], orders[j][level]
            four = slots[j]
            below, above = step(c, 3), step(c, 1)
            arrived(views[j](below), *four[0], me)
            sent.append(send(views[j](below, 0), views[j](below, 0), *four[2], ups[axis]))
            arrived(views[j](above), *four[1], me)
            sent.append(send(views[j](above, 1), views[j](above, 1), *four[3], downs[axis]))
        for j in range(3):
            c = at[orders[j][level]]
            far = step(c, 2)
            arrived(views[j](far, 0), *slots[j][2], me)
            arrived(views[j](far, 1), *slots[j][3], me)

    ring(0, first)
    shared = []
    for j in range(3):
        c = at[orders[j][1]]
        shared.append([(share(j, second[j](c)), c)])
    ring(1, second)
    slots = []
    for j in range(3):
        c, axis = at[orders[j][2]], orders[j][2]
        slots.append([[slot(j) for _ in range(6)], [slot(j) for _ in range(6)]])
    for q in range(4):
        for j in range(3):
            c, axis = at[orders[j][2]], orders[j][2]
            sent.append(send(third[j](c, q), third[j](c, q), *slots[j][0][q], ups[axis]))
            sent.append(send(third[j](c, q), third[j](c, q), *slots[j][1][q], downs[axis]))
    for j in range(3):
        for d in (1, 2, 3):
            c = step(at[orders[j][1]], d)
            shared[j].append((share(j, second[j](c)), c))
    pltpu.make_async_copy(win, win, loc.at[0]).wait()

    started = [False]

    def cells(j, points):
        return [(j, yy, xx) for yy, xx in points]

    def add(points, row_starts, size):
        lhs = jnp.concatenate(
            [jnp.concatenate([pot[j, yy, xx, pl.ds(pl.multiple_of(s, 128), size), :] for s in row_starts], axis=0)
             if len(row_starts) > 1 else pot[j, yy, xx, pl.ds(pl.multiple_of(row_starts[0], 128), size), :]
             for j, yy, xx in points], axis=1)
        rhs = jnp.concatenate([win[(yy * 4 + xx) * 3 + j] for j, yy, xx in points], axis=1)
        value = lax.dot_general(lhs, rhs, (((1,), (1,)), ((), ())), preferred_element_type=F32)
        if not started[0]:
            acc[...] = value
            started[0] = True
            return
        for i, s in enumerate(row_starts):
            where = pl.ds(pl.multiple_of(s, 128), size)
            acc[where, :] += value[i * size:(i + 1) * size]

    whole = [0]
    both = lambda s: [s * 128, 512 + s * 128]

    def twin_done(j, n):
        for i in n:
            sems, c = shared[j][i]
            arrived(second[j](c, kk=1 - k), *sems, me)

    for j in range(3):
        twin_done(j, range(4))
    add(cells(0, [(q, x) for q in range(4)]), [0], 1024)
    late = [[None] * 4 for _ in range(3)]

    def take(q, j):
        c, axis = at[orders[j][2]], orders[j][2]
        below, above = step(c, 3), step(c, 1)
        up, down = slots[j]
        arrived(third[j](below, q), *up[q], me)
        if q < 2:
            sent.append(send(third[j](below, q), third[j](below, q), *up[4 + q], ups[axis]))
        a = share(j, third[j](below, q))
        arrived(third[j](above, q), *down[q], me)
        if q >= 2:
            sent.append(send(third[j](above, q), third[j](above, q), *down[2 + q], downs[axis]))
        b = share(j, third[j](above, q))
        return a, b

    def take_twin(q, j, sems):
        c = at[orders[j][2]]
        arrived(third[j](step(c, 3), q, 1 - k), *sems[0], me)
        arrived(third[j](step(c, 1), q, 1 - k), *sems[1], me)

    pairs = {}
    for q in range(4):
        for j in range(3):
            pairs[q, j] = take(q, j)
        if q == 0:
            add(cells(1, [(y, q) for q in range(4)]), [0], 1024)
        if q == 1:
            add(cells(2, [(a, b) for a in range(4) for b in range(4)]), both(z), 128)
        if q in (1, 3):
            for qq in (q - 1, q):
                for j in range(3):
                    take_twin(qq, j, pairs[qq, j])
            add(cells(0, [(qq, step(x, d)) for qq in (q - 1, q) for d in (1, 3)]), [0], 1024)
            add(cells(1, [(step(y, d), qq) for qq in (q - 1, q) for d in (1, 3)]), [0], 1024)
            add(cells(2, [(qq, b) for qq in (q - 1, q) for b in range(4)]), both(step(z, 1)) + both(step(z, 3)), 128)
    far = {}
    for q in range(4):
        for j in range(3):
            c = step(at[orders[j][2]], 2)
            sems = slots[j][0][4 + q] if q < 2 else slots[j][1][2 + q]
            arrived(third[j](c, q), *sems, me)
            far[q, j] = share(j, third[j](c, q))
    for j in range(3):
        for q in range(4):
            c = step(at[orders[j][2]], 2)
            arrived(third[j](c, q, 1 - k), *far[q, j], me)
    add(cells(0, [(q, step(x, 2)) for q in range(4)]), [0], 1024)
    add(cells(1, [(step(y, 2), q) for q in range(4)]), [0], 1024)
    add(cells(2, [(a, b) for a in range(4) for b in range(4)]), both(step(z, 2)), 128)
    out_ref[...] = acc[...].astype(BF)
    for copy in sent:
        copy.wait_send()


def sems(*shape):
    return pltpu.SemaphoreType.DMA(shape)


ANY = pl.BlockSpec(memory_space=pl.ANY)
VMEM = pl.BlockSpec(memory_space=pltpu.VMEM)


def shards(
    occ_coef, vir_coef, atom_counts, occ_index, vir_index, interaction, window_charges, panel_start
):
    idx = jnp.broadcast_to(jnp.concatenate([occ_index, vir_index])[None], (8, 128))
    block = pl.pallas_call(
        front,
        out_shape=jax.ShapeDtypeStruct((3, 128, 128), BF),
        in_specs=[ANY, ANY, ANY, VMEM, ANY],
        out_specs=VMEM,
        scratch_shapes=[
            pltpu.VMEM((16, 8, 128), jnp.int32),
            pltpu.VMEM((16, 64, 128), BF),
            pltpu.VMEM((16, 128, 128), BF),
            pltpu.VMEM((1024, 1024), BF),
            pltpu.VMEM((1024, 2048), BF),
            pltpu.VMEM((2048, 768), BF),
            pltpu.VMEM((16, 64, 128), BF),
            pltpu.VMEM((16, 64, 128), BF),
            pltpu.VMEM((4, 4, 64, 768), BF),
            pltpu.VMEM((768, 384), BF),
            pltpu.VMEM((512, 384), F32),
            pltpu.VMEM((512, 384), F32),
            pltpu.VMEM((4, 128, 384), F32),
            pltpu.VMEM((4, 2, 128, 384), BF),
            sems(15), sems(16), sems(15), sems(16), sems(15), sems(16), sems(15), sems(16),
            sems(16), sems(16), sems(4), sems(4), sems(1),
        ],
        compiler_params=pltpu.CompilerParams(
            collective_id=0, has_side_effects=True, vmem_limit_bytes=56 * 2**20
        ),
    )(idx, occ_coef, vir_coef, atom_counts, interaction)
    coupling = pl.pallas_call(
        back,
        out_shape=jax.ShapeDtypeStruct((1024, 1024), BF),
        in_specs=[VMEM, ANY],
        out_specs=VMEM,
        scratch_shapes=[
            pltpu.VMEM((3, 4, 4, 1024, 128), BF),
            pltpu.VMEM((48, 1024, 128), BF),
            pltpu.VMEM((1024, 1024), F32),
            sems(3, 20), sems(3, 20), sems(3, 16), sems(3, 16), sems(1),
        ],
        compiler_params=pltpu.CompilerParams(
            collective_id=1, has_side_effects=True, vmem_limit_bytes=56 * 2**20
        ),
    )(block, window_charges)
    panel_index = lax.broadcasted_iota(jnp.int32, coupling.shape, 0)
    window_index = lax.axis_index(("row", "col")) * window_charges.shape[0] + lax.broadcasted_iota(
        jnp.int32, coupling.shape, 1
    )
    upper_mask = window_index >= panel_start[0] + panel_index
    return jnp.where(upper_mask, coupling, jnp.zeros_like(coupling))


def solution(mesh):
    placed = (
        P("row", "col"),
        P("row", "col"),
        P("col", None),
        P("row"),
        P("row"),
        P("col", "row"),
        P(("row", "col"), None),
        P(),
    )
    return jax.shard_map(
        shards, mesh=mesh, in_specs=placed, out_specs=P(None, ("row", "col")), check_vma=False
    )
```

time: 370 us -> 113 us (0.31)
  waiting for transfers between devices: 263 us -> 0 us
  Pallas kernels: 0 us -> 107 us
  blocking collectives: 52 us -> 0 us
  matrix products: 27.1 us -> 0 us
  between operations: 13.8 us -> 0.68 us
  local copies, waits for them, and re-layouts: 9.35 us -> 0.6 us
    all_gather x4 -> x0, waiting for transfers between devices: 262 us -> none  [the longest x1 98 us: shards(): lax.all_gather(summed.astype(jnp.bfloat16), 'row', axis=0, tiled=True)]
    pallas_call x0 -> x2, Pallas kernels: none -> 107 us  [the longest x1 58.1 us: shards(): pl.pallas_call(front, out_shape=jax.ShapeDtypeStruct((3, 128, 128), BF),...]
    psum x1 -> x0, blocking collectives: 52 us -> none  [shards(): summed = lax.psum(partial_value, 'col')]
    dot_general x4 -> x0, matrix products: 27.1 us -> none  [the longest x1 20.2 us: add_rows(): lax.dot_general(block_in, window_charges, (((0,), (1,)), ((), ())), prefe...]
    gather x2 -> x0, local copies, waits for them, and re-layouts: 9.16 us -> none  [the longest x1 5.45 us: shards(): jnp.take(vir_all, vir_index, axis=0).astype(jnp.float32)]
  transfers between devices with their start and end apart: 4 -> 0, of which waited for: 4 -> 0; matrix products, arithmetic and copies ran while one was open for 2% -> 0% of each run, Pallas kernels for 0% -> 0%
where the time goes in v1:
time: 113 us; the launch traced here: 112 us
  Pallas kernels  107 us (95%)
  other arithmetic  4.21 us (4%)
    pallas_call x1, Pallas kernels, shards(): pl.pallas_call(front, out_shape=jax.ShapeDtypeStruct((3, 128, 128), BF),...  58.1 us
    pallas_call x1, Pallas kernels, shards(): pl.pallas_call(back, out_shape=jax.ShapeDtypeStruct((1024, 1024), BF), in...  48.8 us
    select_n x1, other arithmetic, shards(): return jnp.where(upper_mask, coupling, jnp.zeros_like(coupling))  3.46 us

profile of v1, /device:TPU:1, one launch (start us, length us, event | category | flops | bytes accessed | tf_op | source)
XLA Modules:
  0.0 112.4 jit_solution(1745299857436841080)
XLA Ops:
  0.0 0.7 pad_add_fusion
  0.7 0.6 broadcast_in_dim.4.idx_hbm
  1.3 58.1 %shard_map.82.block_ref = bf16[3,128,128]{2,1,0:T(8,128)(2,1)} custom-call(s32[8,128]{1,0:T(8,128)} %broadcast_in_dim.4.idx_hbm, bf16[64,2048]{1,0:T(8,128)(2,1)} %occ_hbm.1, bf16[128,2048]{1,0:T(8,128)(2,1)} %vir_hbm.1, s32[1,768]{1,0:T(1,128)} %counts_ref.1, bf16[768,384]{1,0:T(8,128)(2,1)} %inter_hbm.1), custom_call_target="tpu_custom_call" | custom-call | tf_op jit(solution)/shard_map/pallas_call | solution.py:383
  59.5 48.8 %shard_map.83 = bf16[1024,1024]{1,0:T(8,128)(2,1)} custom-call(bf16[3,128,128]{2,1,0:T(8,128)(2,1)} %shard_map.82.block_ref, bf16[1024,6144]{1,0:T(8,128)(2,1)} %win_hbm.1), custom_call_target="tpu_custom_call" | custom-call | tf_op jit(solution)/shard_map/pallas_call | solution.py:410
  109.0 3.5 %compare_select_fusion = bf16[1024,1024]{1,0:T(8,128)(2,1)} fusion(bf16[1024,1024]{1,0:T(8,128)(2,1)} %shard_map.83, s32[1024]{0:T(1024)S(1)} %get-tuple-element.6, s32[1024]{0:T(1024)S(1)} %get-tuple-element.5), kind=kLoop, calls=%fused_computation | loop fusion | flops 2097152 | bytes 4202496 | tf_op jit(solution)/shard_map/jit(_where)/select_n | solution.py:430
  (1 shorter events, 0.0 us)

commit v2 on v0

v2 whole, which is shorter than its diff:
```python
import jax
import jax.numpy as jnp
from jax import lax
from jax.experimental import pallas as pl
from jax.experimental.pallas import tpu as pltpu
from jax.sharding import PartitionSpec as P

MESH = pl.DeviceIdType.MESH
BF = jnp.bfloat16
F32 = jnp.float32


def place():
    row, col = lax.axis_index("row"), lax.axis_index("col")
    return lax.div(row, 4), lax.rem(row, 4), lax.div(col, 2), lax.rem(col, 2)


def step(c, d):
    return lax.rem(c + d, 4)


def device(y, x, z, k):
    return (y * 4 + x, z * 2 + k)


def send(src, dst, send_sem, recv_sem, target):
    copy = pltpu.make_async_remote_copy(
        src_ref=src, dst_ref=dst, send_sem=send_sem, recv_sem=recv_sem, device_id=target, device_id_type=MESH
    )
    copy.start()
    return copy


def arrived(ref, send_sem, recv_sem, me):
    pltpu.make_async_remote_copy(
        src_ref=ref, dst_ref=ref, send_sem=send_sem, recv_sem=recv_sem, device_id=me, device_id_type=MESH
    ).wait_recv()


def greet(targets):
    barrier = pltpu.get_barrier_semaphore()
    for target in targets:
        pl.semaphore_signal(barrier, inc=1, device_id=target, device_id_type=MESH)
    pl.semaphore_wait(barrier, len(targets))


def iota(shape, dim):
    return lax.broadcasted_iota(jnp.int32, shape, dim).astype(F32)


def panel_kernel(occ_index, vir_index, occ_hbm, vir_hbm, counts_ref, inter_hbm, win_hbm, out_ref,
                 idx_own, idx_all, occ_t, vir_t, pick_occ, pick_vir, member, dens_out, dens, charges_out, charges,
                 inter, half_out, half_in, pot, win, acc,
                 idx_s, idx_r, occ_s, occ_r, vir_s, vir_r, dens_s, dens_r, int_s, int_r, swap_s, swap_r,
                 ag_s, ag_r, half_s, half_r, ici_s, ici_r, d2d_s, d2d_r, loc):
    y, x, z, k = place()
    me = device(y, x, z, k)
    r = y * 4 + x
    twin = device(y, x, z, 1 - k)
    plane = [(step(y, d // 4), step(x, d % 4)) for d in range(1, 16)]
    idx_own[...] = jnp.broadcast_to(jnp.concatenate([occ_index[...], vir_index[...]], axis=1), (8, 128))
    greet(
        [device(yy, xx, z, k) for yy, xx in plane]
        + [device(y, x, step(z, d), k) for d in (1, 2, 3)]
        + [twin]
    )
    ups = {"y": device(step(y, 1), x, z, k), "x": device(y, step(x, 1), z, k), "z": device(y, x, step(z, 1), k)}
    downs = {"y": device(step(y, 3), x, z, k), "x": device(y, step(x, 3), z, k), "z": device(y, x, step(z, 3), k)}
    fars = {"y": device(step(y, 2), x, z, k), "x": device(y, step(x, 2), z, k), "z": device(y, x, step(z, 2), k)}
    at = {"y": y, "x": x, "z": z}
    sent = []
    own_cols = pl.ds(pl.multiple_of(r * 128, 128), 128)
    own_inter = pltpu.make_async_copy(inter_hbm, inter.at[z], loc.at[0])
    for copy in (
        pltpu.make_async_copy(idx_own, idx_all.at[r], idx_r.at[r]),
        pltpu.make_async_copy(occ_hbm.at[:, own_cols], occ_t.at[r], occ_r.at[r]),
        pltpu.make_async_copy(vir_hbm.at[:, own_cols], vir_t.at[r], vir_r.at[r]),
        own_inter,
    ):
        copy.start()
    for d, (yy, xx) in enumerate(plane):
        sent.append(send(idx_own, idx_all.at[r], idx_s.at[d], idx_r.at[r], device(yy, xx, z, k)))
    for d, (yy, xx) in enumerate(plane):
        cols = pl.ds(pl.multiple_of((yy * 4 + xx) * 128, 128), 128)
        sent.append(send(occ_hbm.at[:, cols], occ_t.at[r], occ_s.at[d], occ_r.at[r], device(yy, xx, z, k)))
    for d, (yy, xx) in enumerate(plane):
        cols = pl.ds(pl.multiple_of((yy * 4 + xx) * 128, 128), 128)
        sent.append(send(vir_hbm.at[:, cols], vir_t.at[r], vir_s.at[d], vir_r.at[r], device(yy, xx, z, k)))
    sent.append(send(inter_hbm, inter.at[z], int_s.at[0], int_r.at[0], ups["z"]))
    sent.append(send(inter_hbm, inter.at[z], int_s.at[1], int_r.at[1], downs["z"]))
    counts = counts_ref[...].astype(F32)
    upper = (iota((768, 768), 0) <= iota((768, 768), 1)).astype(BF)
    ends = jnp.dot(jnp.broadcast_to(counts, (8, 768)).astype(BF), upper, preferred_element_type=F32)[0:1]
    starts = ends - counts

    def members(i, carry):
        basis = iota((256, 768), 0) + (i * 256).astype(F32)
        inside = jnp.logical_and(basis >= starts, basis < ends)
        member[pl.ds(pl.multiple_of(i * 256, 256), 256), :] = jnp.where(inside, 1.0, 0.0).astype(BF)
        return carry

    lax.fori_loop(0, 8, members, 0)
    for s in range(16):
        arrived(idx_all.at[s], idx_s.at[0], idx_r.at[s], me)

    def picks(s, carry):
        line = idx_all[s][0:1].astype(F32)
        mine = iota((128, 128), 0) == iota((128, 128), 1)
        column = jnp.sum(jnp.where(mine, jnp.broadcast_to(line, (128, 128)), 0.0), axis=1, keepdims=True)
        rows = pl.ds(pl.multiple_of(s * 64, 64), 64)
        pick_occ[rows, :] = jnp.where(column[0:64] == iota((64, 1024), 1), 1.0, 0.0).astype(BF)
        pick_vir[rows, :] = jnp.where(column[64:128] == iota((64, 2048), 1), 1.0, 0.0).astype(BF)
        return carry

    lax.fori_loop(0, 16, picks, 0)
    for s in range(16):
        arrived(occ_t.at[s], occ_s.at[0], occ_r.at[s], me)
    for s in range(16):
        arrived(vir_t.at[s], vir_s.at[0], vir_r.at[s], me)
    occ_rows, vir_rows = occ_t[...].reshape(1024, 128), vir_t[...].reshape(2048, 128)
    n = 0
    for dy in (2, 1, 3, 0):
        yy = step(y, dy)
        rows = pl.ds(pl.multiple_of(yy * 256, 256), 256)
        first_rows = jnp.dot(pick_occ[rows, :], occ_rows, preferred_element_type=F32)
        second_rows = jnp.dot(pick_vir[rows, :], vir_rows, preferred_element_type=F32)
        dens_out[pl.ds(yy * 4, 4)] = (first_rows * second_rows).astype(BF).reshape(4, 64, 128)
        for dx in (2, 1, 3, 0):
            xx = step(x, dx)
            other = yy * 4 + xx
            if dy == 0 and dx == 0:
                pltpu.make_async_copy(dens_out.at[r], dens.at[r], dens_r.at[r]).start()
            else:
                sent.append(send(dens_out.at[other], dens.at[r], dens_s.at[n], dens_r.at[r], device(yy, xx, z, k)))
                n += 1

    def load(i, carry):
        cols = pl.ds(pl.multiple_of(i * 128, 128), 128)
        pltpu.make_async_copy(win_hbm.at[:, cols], win.at[i], loc.at[1]).start()
        return carry

    lax.fori_loop(0, 48, load, 0)
    for s in range(16):
        arrived(dens.at[s], dens_s.at[0], dens_r.at[s], me)
    density = jnp.concatenate([dens[s] for s in range(16)], axis=1)
    own_charges = jnp.dot(density, member[...], preferred_element_type=F32).astype(BF)
    charges_out[...] = own_charges.reshape(4, 16, 768)
    charges[y, x, z] = charges_out[z]
    for d in (1, 2, 3):
        zz = step(z, d)
        sent.append(send(charges_out.at[zz], charges.at[y, x, z], swap_s.at[d], swap_r.at[d], device(y, x, zz, k)))
    below, above = step(z, 3), step(z, 1)
    arrived(inter.at[below], int_s.at[0], int_r.at[0], me)
    top, bottom = pl.ds(0, 384), pl.ds(384, 384)
    sent.append(send(inter.at[below, top], inter.at[below, top], int_s.at[2], int_r.at[2], ups["z"]))
    arrived(inter.at[above], int_s.at[1], int_r.at[1], me)
    sent.append(send(inter.at[above, bottom], inter.at[above, bottom], int_s.at[3], int_r.at[3], downs["z"]))
    for d in (1, 2, 3):
        arrived(charges.at[y, x, step(z, 4 - d)], swap_s.at[d], swap_r.at[d], me)
    views = (
        lambda a, b, h=None: charges.at[b, a, pl.ds(0, 2)],
        lambda a, b, h=None: charges.at[a, b, pl.ds(2, 2)],
    )
    axes = (("x", "y"), ("y", "x"))

    def plane_sems(part, i):
        return ag_s.at[part, i], ag_r.at[part, i]

    def plane_block(part, a, b):
        return views[part](step(at[axes[part][0]], a), step(at[axes[part][1]], b))

    def plane_second(part, a):
        ref = plane_block(part, a, 0)
        sent.append(send(ref, ref, *plane_sems(part, 3 + a), ups[axes[part][1]]))
        sent.append(send(ref, ref, *plane_sems(part, 7 + a), downs[axes[part][1]]))

    def plane_first_arrival(part, a):
        arrived(plane_block(part, a, 0), *plane_sems(part, {3: 0, 1: 1, 2: 2}[a]), me)
        plane_second(part, a)

    def plane_second_arrival(part, a):
        ref = plane_block(part, a, 3)
        arrived(ref, *plane_sems(part, 3 + a), me)
        if a in (0, 2):
            sent.append(send(ref, ref, *plane_sems(part, 11 + a), ups[axes[part][1]]))
        ref = plane_block(part, a, 1)
        arrived(ref, *plane_sems(part, 7 + a), me)
        if a in (1, 3):
            sent.append(send(ref, ref, *plane_sems(part, 11 + a), downs[axes[part][1]]))

    for part in range(2):
        ref = plane_block(part, 0, 0)
        sent.append(send(ref, ref, *plane_sems(part, 0), ups[axes[part][0]]))
        sent.append(send(ref, ref, *plane_sems(part, 1), downs[axes[part][0]]))
        sent.append(send(ref, ref, *plane_sems(part, 2), fars[axes[part][0]]))
    for part in range(2):
        plane_second(part, 0)
    for what, a in ((1, 3), (1, 1), (2, 0), (1, 2), (2, 3), (2, 1), (2, 2)):
        for part in range(2):
            (plane_first_arrival if what == 1 else plane_second_arrival)(part, a)
    for a in range(4):
        for part in range(2):
            arrived(plane_block(part, a, 2), *plane_sems(part, 11 + a), me)
    own_inter.wait()
    arrived(inter.at[step(z, 2), top], int_s.at[2], int_r.at[2], me)
    arrived(inter.at[step(z, 2), bottom], int_s.at[3], int_r.at[3], me)

    def product(half):
        lhs = jnp.concatenate([charges[pl.ds(2 * half, 2), :, zz].reshape(128, 768) for zz in range(4)], axis=1)
        return jnp.dot(lhs, inter[...].reshape(3072, 384), preferred_element_type=F32)

    half_out[...] = product(1 - k)
    swap = send(half_out, half_in, half_s.at[0], half_r.at[0], twin)
    sent.append(swap)
    total = product(k)
    swap.wait_recv()
    total = (total + half_in[...]).astype(BF)

    def rows(s, kk=k, n=128):
        return pl.ds(pl.multiple_of(kk * 512 + s * 128, 128), n)

    def half_rows(kk=k):
        return pl.ds(pl.multiple_of(kk * 512, 512), 512)

    for j in range(3):
        pot[j, y, x, rows(z), :] = total[:, 128 * j:128 * j + 128]
    orders = ("zyx", "xzy", "yxz")
    first = (
        lambda s: pot.at[0, y, x, rows(s)],
        lambda s: pot.at[1, y, s, rows(z)],
        lambda s: pot.at[2, s, x, rows(z)],
    )

    def two(h):
        return slice(None) if h is None else pl.ds(2 * h, 2)

    second = (
        lambda s, h=None, kk=k: pot.at[0, s, x, half_rows(kk) if h is None else pl.ds(pl.multiple_of(kk * 512 + 256 * h, 256), 256)],
        lambda s, h=None, kk=k: pot.at[1, y, two(h), rows(s, kk)],
        lambda s, h=None, kk=k: pot.at[2, two(h), s, rows(z, kk)],
    )
    third = (
        lambda s, q, kk=k: pot.at[0, q, s, half_rows(kk)],
        lambda s, q, kk=k: pot.at[1, s, :, rows(q, kk)],
        lambda s, q, kk=k: pot.at[2, :, q, rows(s, kk)],
    )
    n_d2d = [0, 0, 0]

    def ici(j, i):
        return ici_s.at[j, i], ici_r.at[j, i]

    def share(j, ref):
        n_d2d[j] += 1
        pair = d2d_s.at[j, n_d2d[j] - 1], d2d_r.at[j, n_d2d[j] - 1]
        sent.append(send(ref, ref, *pair, twin))
        return pair

    c1, c2, c3 = ([at[orders[j][level]] for j in range(3)] for level in range(3))
    shared, chunks = {}, {}

    def third_send(j, a):
        ref = third[j](c3[j], step(c2[j], a))
        sent.append(send(ref, ref, *ici(j, 7 + a), ups[orders[j][2]]))
        sent.append(send(ref, ref, *ici(j, 11 + a), downs[orders[j][2]]))

    def third_arrival(a):
        for j in range(3):
            q = step(c2[j], a)
            ref = third[j](step(c3[j], 3), q)
            arrived(ref, *ici(j, 7 + a), me)
            if a in (0, 2):
                sent.append(send(ref, ref, *ici(j, 15 + a), ups[orders[j][2]]))
            chunks[j, a, 3] = share(j, ref)
            ref = third[j](step(c3[j], 1), q)
            arrived(ref, *ici(j, 11 + a), me)
            if a in (1, 3):
                sent.append(send(ref, ref, *ici(j, 15 + a), downs[orders[j][2]]))
            chunks[j, a, 1] = share(j, ref)

    def far_arrival(a):
        for j in range(3):
            ref = third[j](step(c3[j], 2), step(c2[j], a))
            arrived(ref, *ici(j, 15 + a), me)
            chunks[j, a, 2] = share(j, ref)

    def second_twin(j):
        for a in range(4):
            arrived(second[j](step(c2[j], a), kk=1 - k), *shared[j, a], me)

    def chunk_twin(j, a, b):
        arrived(third[j](step(c3[j], b), step(c2[j], a), 1 - k), *chunks[j, a, b], me)

    for j in range(3):
        ref = first[j](c1[j])
        sent.append(send(ref, ref, *ici(j, 0), ups[orders[j][0]]))
        sent.append(send(ref, ref, *ici(j, 1), downs[orders[j][0]]))
        sent.append(send(ref, ref, *ici(j, 2), fars[orders[j][0]]))
    pltpu.make_async_copy(win, win, loc.at[1]).wait()
    for j in range(3):
        for i, d in enumerate((3, 1, 2)):
            arrived(first[j](step(c1[j], d)), *ici(j, i), me)
        ref = second[j](c2[j])
        sent.append(send(ref, ref, *ici(j, 3), ups[orders[j][1]]))
        sent.append(send(ref, ref, *ici(j, 4), downs[orders[j][1]]))
        third_send(j, 0)
        shared[j, 0] = share(j, ref)
    for j in range(3):
        ref = second[j](step(c2[j], 3))
        arrived(ref, *ici(j, 3), me)
        half = second[j](step(c2[j], 3), 0)
        sent.append(send(half, half, *ici(j, 5), ups[orders[j][1]]))
        third_send(j, 3)
        shared[j, 3] = share(j, ref)
        ref = second[j](step(c2[j], 1))
        arrived(ref, *ici(j, 4), me)
        half = second[j](step(c2[j], 1), 1)
        sent.append(send(half, half, *ici(j, 6), downs[orders[j][1]]))
        third_send(j, 1)
        shared[j, 1] = share(j, ref)
    third_arrival(0)
    for j in range(3):
        far = step(c2[j], 2)
        arrived(second[j](far, 0), *ici(j, 5), me)
        arrived(second[j](far, 1), *ici(j, 6), me)
        third_send(j, 2)
        shared[j, 2] = share(j, second[j](far))

    started = [False]

    def add(points, row_starts, size):
        lhs = jnp.concatenate([
            jnp.concatenate([pot[j, yy, xx, pl.ds(pl.multiple_of(s, 128), size), :] for s in row_starts], axis=0)
            for j, yy, xx in points], axis=1)
        rhs = jnp.concatenate([win[(yy * 4 + xx) * 3 + j] for j, yy, xx in points], axis=1)
        value = lax.dot_general(lhs, rhs, (((1,), (1,)), ((), ())), preferred_element_type=F32)
        if not started[0]:
            acc[...] = value
            started[0] = True
            return
        for i, s in enumerate(row_starts):
            where = pl.ds(pl.multiple_of(s, 128), size)
            acc[where, :] += value[i * size:(i + 1) * size]

    def both(s):
        return [s * 128, 512 + s * 128]

    def add_second(j):
        second_twin(j)
        if j == 0:
            add([(0, q, x) for q in range(4)], [0], 1024)
        if j == 1:
            add([(1, y, q) for q in range(4)], [0], 1024)
        if j == 2:
            add([(2, a, b) for a in range(4) for b in range(4)], both(z), 128)

    def add_third(j, chunk_pair, others):
        for a in chunk_pair:
            for b in others:
                chunk_twin(j, a, b)
        qs = [step(c2[j], a) for a in chunk_pair]
        ss = [step(c3[j], b) for b in others]
        if j == 0:
            add([(0, q, s) for q in qs for s in ss], [0], 1024)
        if j == 1:
            add([(1, s, b) for s in ss for b in range(4)], both(qs[0]) + both(qs[1]), 128)
        if j == 2:
            add([(2, a, q) for a in range(4) for q in qs], [v for s in ss for v in both(s)], 128)

    add_second(0)
    third_arrival(3)
    add_second(1)
    add_second(2)
    third_arrival(1)
    add_third(0, (0, 3), (3, 1))
    add_third(1, (0, 3), (3, 1))
    third_arrival(2)
    add_third(2, (0, 3), (3, 1))
    far_arrival(0)
    far_arrival(3)
    for j in range(3):
        add_third(j, (1, 2), (3, 1))
    far_arrival(1)
    far_arrival(2)
    for j in range(3):
        add_third(j, (0, 3), (2,))
    for j in range(3):
        add_third(j, (1, 2), (2,))
    for kk in range(2):
        for zz in range(4):
            for i in range(8):
                out_ref[(kk * 8 + i) * 64 + zz * 16:(kk * 8 + i) * 64 + zz * 16 + 16] = acc[
                    kk * 512 + zz * 128 + i * 16:kk * 512 + zz * 128 + i * 16 + 16].astype(BF)
    for copy in sent:
        copy.wait_send()


def sems(*shape):
    return pltpu.SemaphoreType.DMA(shape)


ANY = pl.BlockSpec(memory_space=pl.ANY)
VMEM = pl.BlockSpec(memory_space=pltpu.VMEM)


def shards(
    occ_coef, vir_coef, atom_counts, occ_index, vir_index, interaction, window_charges, panel_start
):
    coupling = pl.pallas_call(
        panel_kernel,
        out_shape=jax.ShapeDtypeStruct((1024, 1024), BF),
        in_specs=[VMEM, VMEM, ANY, ANY, VMEM, ANY, ANY],
        out_specs=VMEM,
        scratch_shapes=[
            pltpu.VMEM((8, 128), jnp.int32),
            pltpu.VMEM((16, 8, 128), jnp.int32),
            pltpu.VMEM((16, 64, 128), BF),
            pltpu.VMEM((16, 128, 128), BF),
            pltpu.VMEM((1024, 1024), BF),
            pltpu.VMEM((1024, 2048), BF),
            pltpu.VMEM((2048, 768), BF),
            pltpu.VMEM((16, 64, 128), BF),
            pltpu.VMEM((16, 64, 128), BF),
            pltpu.VMEM((4, 16, 768), BF),
            pltpu.VMEM((4, 4, 4, 16, 768), BF),
            pltpu.VMEM((4, 768, 384), BF),
            pltpu.VMEM((128, 384), F32),
            pltpu.VMEM((128, 384), F32),
            pltpu.VMEM((3, 4, 4, 1024, 128), BF),
            pltpu.VMEM((48, 1024, 128), BF),
            pltpu.VMEM((1024, 1024), F32),
            sems(15), sems(16), sems(15), sems(16), sems(15), sems(16), sems(15), sems(16),
            sems(4), sems(4), sems(4), sems(4), sems(2, 15), sems(2, 15), sems(1), sems(1),
            sems(3, 19), sems(3, 19), sems(3, 16), sems(3, 16), sems(2),
        ],
        compiler_params=pltpu.CompilerParams(
            collective_id=0, has_side_effects=True, vmem_limit_bytes=60 * 2**20
        ),
    )(occ_index[None], vir_index[None], occ_coef, vir_coef, atom_counts, interaction, window_charges)
    panel_index = lax.broadcasted_iota(jnp.int32, coupling.shape, 0)
    window_index = lax.axis_index(("row", "col")) * window_charges.shape[0] + lax.broadcasted_iota(
        jnp.int32, coupling.shape, 1
    )
    upper_mask = window_index >= panel_start[0] + panel_index
    return jnp.where(upper_mask, coupling, jnp.zeros_like(coupling))


def solution(mesh):
    placed = (
        P("row", "col"),
        P("row", "col"),
        P("col", None),
        P("row"),
        P("row"),
        P("col", "row"),
        P(("row", "col"), None),
        P(),
    )
    return jax.shard_map(
        shards, mesh=mesh, in_specs=placed, out_specs=P(None, ("row", "col")), check_vma=False
    )
```

time: 370 us -> 94.2 us (0.25)
  waiting for transfers between devices: 263 us -> 0 us
  Pallas kernels: 0 us -> 89.9 us
  blocking collectives: 52 us -> 0 us
  matrix products: 27.1 us -> 0 us
  between operations: 13.8 us -> 0.67 us
  local copies, waits for them, and re-layouts: 9.35 us -> 0 us
    all_gather x4 -> x0, waiting for transfers between devices: 262 us -> none  [the longest x1 98 us: shards(): lax.all_gather(summed.astype(jnp.bfloat16), 'row', axis=0, tiled=True)]
    pallas_call x0 -> x1, Pallas kernels: none -> 89.9 us  [shards(): pl.pallas_call(panel_kernel, out_shape=jax.ShapeDtypeStruct((1024, 1024),...]
    psum x1 -> x0, blocking collectives: 52 us -> none  [shards(): summed = lax.psum(partial_value, 'col')]
    dot_general x4 -> x0, matrix products: 27.1 us -> none  [the longest x1 20.2 us: add_rows(): lax.dot_general(block_in, window_charges, (((0,), (1,)), ((), ())), prefe...]
    gather x2 -> x0, local copies, waits for them, and re-layouts: 9.16 us -> none  [the longest x1 5.45 us: shards(): jnp.take(vir_all, vir_index, axis=0).astype(jnp.float32)]
  transfers between devices with their start and end apart: 4 -> 0, of which waited for: 4 -> 0; matrix products, arithmetic and copies ran while one was open for 2% -> 0% of each run, Pallas kernels for 0% -> 0%
where the time goes in v2:
time: 94.2 us; the launch traced here: 94 us
  Pallas kernels  89.9 us (95%)
  other arithmetic  3.46 us (4%)
    pallas_call x1, Pallas kernels, shards(): pl.pallas_call(panel_kernel, out_shape=jax.ShapeDtypeStruct((1024, 1024),...  89.9 us
    select_n x1, other arithmetic, shards(): return jnp.where(upper_mask, coupling, jnp.zeros_like(coupling))  3.46 us

profile of v2, /device:TPU:1, one launch (start us, length us, event | category | flops | bytes accessed | tf_op | source)
XLA Modules:
  0.0 94.0 jit_solution(17008990562078777806)
XLA Ops:
  0.7 89.9 %shard_map.82 = bf16[1024,1024]{1,0:T(8,128)(2,1)} custom-call(s32[1,64]{1,0:T(1,128)} %bitcast.4, s32[1,64]{1,0:T(1,128)} %bitcast.5, bf16[64,2048]{1,0:T(8,128)(2,1)} %occ_hbm.1, bf16[128,2048]{1,0:T(8,128)(2,1)} %vir_hbm.1, s32[1,768]{1,0:T(1,128)} %counts_ref.1, bf16[768,384]{1,0:T(8,128)(2,1)} %inter_hbm.1, bf16[1024,6144]{1,0:T(8,128)(2,1)} %win_hbm.1), custom_call_target="tpu_custom_call" | custom-call | tf_op jit(solution)/shard_map/pallas_call | solution.py:408
  90.5 3.5 %compare_select_fusion = bf16[1024,1024]{1,0:T(8,128)(2,1)} fusion(bf16[1024,1024]{1,0:T(8,128)(2,1)} %shard_map.82, s32[1024]{0:T(1024)S(1)} %get-tuple-element.6, s32[1024]{0:T(1024)S(1)} %get-tuple-element.5), kind=kLoop, calls=%fused_computation | loop fusion | flops 2097152 | bytes 4202496 | tf_op jit(solution)/shard_map/jit(_where)/select_n | solution.py:444
  (1 shorter events, 0.0 us)

commit v3 on v2

v3 whole, which is shorter than its diff:
```python
import jax
import jax.numpy as jnp
from jax import lax
from jax.experimental import pallas as pl
from jax.experimental.pallas import tpu as pltpu
from jax.sharding import PartitionSpec as P

MESH = pl.DeviceIdType.MESH
BF = jnp.bfloat16
F32 = jnp.float32


def place():
    row, col = lax.axis_index("row"), lax.axis_index("col")
    return lax.div(row, 4), lax.rem(row, 4), lax.div(col, 2), lax.rem(col, 2)


def step(c, d):
    return lax.rem(c + d, 4)


def device(y, x, z, k):
    return (y * 4 + x, z * 2 + k)


def send(src, dst, send_sem, recv_sem, target):
    copy = pltpu.make_async_remote_copy(
        src_ref=src, dst_ref=dst, send_sem=send_sem, recv_sem=recv_sem, device_id=target, device_id_type=MESH
    )
    copy.start()


def left(ref, send_sem, me):
    pltpu.make_async_remote_copy(
        src_ref=ref, dst_ref=ref, send_sem=send_sem, recv_sem=send_sem, device_id=me, device_id_type=MESH
    ).wait_send()


def arrived(ref, send_sem, recv_sem, me):
    pltpu.make_async_remote_copy(
        src_ref=ref, dst_ref=ref, send_sem=send_sem, recv_sem=recv_sem, device_id=me, device_id_type=MESH
    ).wait_recv()


def iota(shape, dim):
    return lax.broadcasted_iota(jnp.int32, shape, dim).astype(F32)


def panel_kernel(occ_index, vir_index, occ_hbm, vir_hbm, counts_hbm, inter_hbm, win_hbm, out_ref,
                 occ_own, vir_own, counts_ref, idx_own, idx_all, occ_t, vir_t, pick_occ, pick_vir, picked_occ, picked_vir, member, dens_out, dens, charges_out, charges,
                 inter, halves, half_in, pot, win, acc,
                 idx_s, idx_r, occ_s, occ_r, vir_s, vir_r, dens_s, dens_r, int_s, int_r, swap_s, swap_r,
                 ag_s, ag_r, half_s, half_r, ici_s, ici_r, d2d_s, d2d_r, loc):
    y, x, z, k = place()
    me = device(y, x, z, k)
    r = y * 4 + x
    twin = device(y, x, z, 1 - k)
    plane = [(step(y, dy), step(x, dx)) for dy in (0, 1, 3, 2) for dx in range(4) if dy or dx]
    small = [
        pltpu.make_async_copy(occ_index, occ_own, loc.at[2]),
        pltpu.make_async_copy(vir_index, vir_own, loc.at[3]),
        pltpu.make_async_copy(counts_hbm, counts_ref, loc.at[4]),
    ]
    for copy in small:
        copy.start()
    partners = (
        [device(yy, xx, z, k) for yy, xx in plane]
        + [device(y, x, step(z, d), k) for d in (1, 2, 3)]
        + [twin]
    )
    barrier = pltpu.get_barrier_semaphore()
    for target in partners:
        pl.semaphore_signal(barrier, inc=1, device_id=target, device_id_type=MESH)
    for copy in small:
        copy.wait()
    idx_own[...] = jnp.broadcast_to(jnp.concatenate([occ_own[...], vir_own[...]], axis=1), (8, 128))
    pl.semaphore_wait(barrier, len(partners))
    ups = {"y": device(step(y, 1), x, z, k), "x": device(y, step(x, 1), z, k), "z": device(y, x, step(z, 1), k)}
    downs = {"y": device(step(y, 3), x, z, k), "x": device(y, step(x, 3), z, k), "z": device(y, x, step(z, 3), k)}
    fars = {"y": device(step(y, 2), x, z, k), "x": device(y, step(x, 2), z, k), "z": device(y, x, step(z, 2), k)}
    at = {"y": y, "x": x, "z": z}
    own_cols = pl.ds(pl.multiple_of(r * 128, 128), 128)
    own_inter = pltpu.make_async_copy(inter_hbm, inter.at[z], loc.at[0])
    for copy in (
        pltpu.make_async_copy(idx_own, idx_all.at[r], idx_r.at[0]),
        pltpu.make_async_copy(occ_hbm.at[:, own_cols], occ_t.at[r], occ_r.at[0]),
        pltpu.make_async_copy(vir_hbm.at[:, own_cols], vir_t.at[r], vir_r.at[y]),
        own_inter,
    ):
        copy.start()
    for d, (yy, xx) in enumerate(plane):
        send(idx_own, idx_all.at[r], idx_s.at[0], idx_r.at[0], device(yy, xx, z, k))
    for d, (yy, xx) in enumerate(plane):
        cols = pl.ds(pl.multiple_of((yy * 4 + xx) * 128, 128), 128)
        send(occ_hbm.at[:, cols], occ_t.at[r], occ_s.at[0], occ_r.at[0], device(yy, xx, z, k))
    for d, (yy, xx) in enumerate(plane):
        cols = pl.ds(pl.multiple_of((yy * 4 + xx) * 128, 128), 128)
        send(vir_hbm.at[:, cols], vir_t.at[r], vir_s.at[0], vir_r.at[y], device(yy, xx, z, k))
    send(inter_hbm, inter.at[z], int_s.at[0], int_r.at[0], ups["z"])
    send(inter_hbm, inter.at[z], int_s.at[0], int_r.at[1], downs["z"])
    def load(i, carry):
        cols = pl.ds(pl.multiple_of(i * 128, 128), 128)
        pltpu.make_async_copy(win_hbm.at[:, cols], win.at[i], loc.at[1]).start()
        return carry

    lax.fori_loop(0, 48, load, 0)
    counts = counts_ref[...].astype(F32)
    upper = (iota((768, 768), 0) <= iota((768, 768), 1)).astype(BF)
    ends = jnp.dot(jnp.broadcast_to(counts, (8, 768)).astype(BF), upper, preferred_element_type=F32)[0:1]
    starts = ends - counts

    def members(i, carry):
        basis = iota((256, 768), 0) + (i * 256).astype(F32)
        inside = jnp.logical_and(basis >= starts, basis < ends)
        member[pl.ds(pl.multiple_of(i * 256, 256), 256), :] = jnp.where(inside, 1.0, 0.0).astype(BF)
        return carry

    lax.fori_loop(0, 8, members, 0)
    arrived(idx_all, idx_s.at[0], idx_r.at[0], me)

    def picks(s, carry):
        line = idx_all[s][0:1].astype(F32)
        mine = iota((128, 128), 0) == iota((128, 128), 1)
        column = jnp.sum(jnp.where(mine, jnp.broadcast_to(line, (128, 128)), 0.0), axis=1, keepdims=True)
        rows = pl.ds(pl.multiple_of(s * 64, 64), 64)
        pick_occ[rows, :] = jnp.where(column[0:64] == iota((64, 1024), 1), 1.0, 0.0).astype(BF)
        pick_vir[rows, :] = jnp.where(column[64:128] == iota((64, 2048), 1), 1.0, 0.0).astype(BF)
        return carry

    lax.fori_loop(0, 16, picks, 0)
    arrived(occ_t, occ_s.at[0], occ_r.at[0], me)
    picked_occ[...] = jnp.dot(pick_occ[...], occ_t[...].reshape(1024, 128), preferred_element_type=F32)

    def vir_line(rows, yy):
        cols = pl.ds(pl.multiple_of(yy * 512, 512), 512)
        return jnp.dot(
            pick_vir[rows, cols], vir_t[pl.ds(yy * 4, 4)].reshape(512, 128), preferred_element_type=F32
        )

    for i, dy in enumerate((0, 3, 1, 2)):
        yy = step(y, dy)
        arrived(vir_t.at[pl.ds(yy * 4, 4)], vir_s.at[0], vir_r.at[yy], me)
        if i == 0:
            picked_vir[...] = vir_line(slice(None), yy)
        elif i < 3:
            picked_vir[...] += vir_line(slice(None), yy)
    for dy in (2, 1, 3, 0):
        yy = step(y, dy)
        rows = pl.ds(pl.multiple_of(yy * 256, 256), 256)
        second_rows = picked_vir[rows, :] + vir_line(rows, step(y, 2))
        dens_out[pl.ds(yy * 4, 4)] = (picked_occ[rows, :] * second_rows).astype(BF).reshape(4, 64, 128)
        for dx in (2, 1, 3, 0):
            xx = step(x, dx)
            other = yy * 4 + xx
            if dy == 0 and dx == 0:
                pltpu.make_async_copy(dens_out.at[r], dens.at[r], dens_r.at[0]).start()
            else:
                send(dens_out.at[other], dens.at[r], dens_s.at[0], dens_r.at[0], device(yy, xx, z, k))

    left(idx_all.at[pl.ds(0, 15)], idx_s.at[0], me)
    left(occ_t.at[pl.ds(0, 15)], occ_s.at[0], me)
    left(vir_t.at[pl.ds(0, 15)], vir_s.at[0], me)
    arrived(dens, dens_s.at[0], dens_r.at[0], me)
    density = jnp.concatenate([dens[s] for s in range(16)], axis=1)
    own_charges = jnp.dot(density, member[...], preferred_element_type=F32).astype(BF)
    charges_out[...] = own_charges.reshape(4, 16, 768)
    charges[y, x, z] = charges_out[z]
    for d in (1, 2, 3):
        zz = step(z, d)
        send(charges_out.at[zz], charges.at[y, x, z], swap_s.at[0], swap_r.at[0], device(y, x, zz, k))
    below, above = step(z, 3), step(z, 1)
    arrived(inter.at[below], int_s.at[0], int_r.at[0], me)
    top, bottom = pl.ds(0, 384), pl.ds(384, 384)
    send(inter.at[below, top], inter.at[below, top], int_s.at[0], int_r.at[2], ups["z"])
    arrived(inter.at[above], int_s.at[0], int_r.at[1], me)
    send(inter.at[above, bottom], inter.at[above, bottom], int_s.at[0], int_r.at[3], downs["z"])
    left(dens.at[pl.ds(0, 15)], dens_s.at[0], me)
    arrived(charges_out.at[pl.ds(0, 3)], swap_s.at[0], swap_r.at[0], me)
    views = (
        lambda a, b, h=None: charges.at[b, a, pl.ds(0, 2)],
        lambda a, b, h=None: charges.at[a, b, pl.ds(2, 2)],
    )
    axes = (("x", "y"), ("y", "x"))

    def plane_sems(part, i):
        return ag_s.at[0], ag_r.at[part, i]

    def plane_block(part, a, b):
        return views[part](step(at[axes[part][0]], a), step(at[axes[part][1]], b))

    def plane_second(part, a):
        ref = plane_block(part, a, 0)
        send(ref, ref, *plane_sems(part, 3 + a), ups[axes[part][1]])
        send(ref, ref, *plane_sems(part, 7 + a), downs[axes[part][1]])

    def plane_first_arrival(part, a):
        arrived(plane_block(part, a, 0), *plane_sems(part, {3: 0, 1: 1, 2: 2}[a]), me)
        plane_second(part, a)

    def plane_second_arrival(part, a):
        ref = plane_block(part, a, 3)
        arrived(ref, *plane_sems(part, 3 + a), me)
        if a in (0, 2):
            send(ref, ref, *plane_sems(part, 11), ups[axes[part][1]])
        ref = plane_block(part, a, 1)
        arrived(ref, *plane_sems(part, 7 + a), me)
        if a in (1, 3):
            send(ref, ref, *plane_sems(part, 11), downs[axes[part][1]])

    for part in range(2):
        ref = plane_block(part, 0, 0)
        send(ref, ref, *plane_sems(part, 0), ups[axes[part][0]])
        send(ref, ref, *plane_sems(part, 1), downs[axes[part][0]])
        send(ref, ref, *plane_sems(part, 2), fars[axes[part][0]])
    for part in range(2):
        plane_second(part, 0)
    for what, a in ((1, 3), (1, 1), (2, 0), (1, 2), (2, 3), (2, 1), (2, 2)):
        for part in range(2):
            (plane_first_arrival if what == 1 else plane_second_arrival)(part, a)
    left(charges_out.at[pl.ds(0, 3)], swap_s.at[0], me)
    arrived(charges.at[step(y, 2), :, pl.ds(0, 2)], *plane_sems(0, 11), me)
    arrived(charges.at[:, step(x, 2), pl.ds(2, 2)], *plane_sems(1, 11), me)
    own_inter.wait()
    arrived(inter.at[step(z, 2), top], int_s.at[0], int_r.at[2], me)
    arrived(inter.at[step(z, 2), bottom], int_s.at[0], int_r.at[3], me)

    lhs = jnp.concatenate([charges[:, :, zz].reshape(256, 768) for zz in range(4)], axis=1)
    halves[...] = jnp.dot(lhs, inter[...].reshape(3072, 384), preferred_element_type=F32).reshape(2, 128, 384)
    send(halves.at[1 - k], half_in, half_s.at[0], half_r.at[0], twin)
    left(inter.at[pl.ds(0, 3)], int_s.at[0], me)
    left(pot.at[0, pl.ds(0, 3), pl.ds(0, 3), pl.ds(0, 640)], ag_s.at[0], me)
    arrived(half_in, half_s.at[0], half_r.at[0], me)
    total = (halves[k] + half_in[...]).astype(BF)

    def rows(s, kk=k, n=128):
        return pl.ds(pl.multiple_of(kk * 512 + s * 128, 128), n)

    def half_rows(kk=k):
        return pl.ds(pl.multiple_of(kk * 512, 512), 512)

    for j in range(3):
        pot[j, y, x, rows(z), :] = total[:, 128 * j:128 * j + 128]
    orders = ("zyx", "xzy", "yxz")
    first = (
        lambda s: pot.at[0, y, x, rows(s)],
        lambda s: pot.at[1, y, s, rows(z)],
        lambda s: pot.at[2, s, x, rows(z)],
    )

    def two(h):
        return slice(None) if h is None else pl.ds(2 * h, 2)

    second = (
        lambda s, h=None, kk=k: pot.at[0, s, x, half_rows(kk) if h is None else pl.ds(pl.multiple_of(kk * 512 + 256 * h, 256), 256)],
        lambda s, h=None, kk=k: pot.at[1, y, two(h), rows(s, kk)],
        lambda s, h=None, kk=k: pot.at[2, two(h), s, rows(z, kk)],
    )
    third = (
        lambda s, q, kk=k: pot.at[0, q, s, half_rows(kk)],
        lambda s, q, kk=k: pot.at[1, s, :, rows(q, kk)],
        lambda s, q, kk=k: pot.at[2, :, q, rows(s, kk)],
    )

    def ici(j, i):
        return ici_s.at[0], ici_r.at[j, i]

    def share(j, ref, group):
        send(ref, ref, d2d_s.at[0], d2d_r.at[j, group], twin)

    def shared(j, group, ref):
        arrived(ref, d2d_s.at[0], d2d_r.at[j, group], me)

    def chunk_group(a, b):
        return 1 + (a in (1, 2)) + 2 * (b == 2)

    c1, c2, c3 = ([at[orders[j][level]] for j in range(3)] for level in range(3))

    def third_send(j, a):
        ref = third[j](c3[j], step(c2[j], a))
        send(ref, ref, *ici(j, 7 + a), ups[orders[j][2]])
        send(ref, ref, *ici(j, 11 + a), downs[orders[j][2]])

    def third_arrival(a):
        for j in range(3):
            q = step(c2[j], a)
            ref = third[j](step(c3[j], 3), q)
            arrived(ref, *ici(j, 7 + a), me)
            if a in (0, 2):
                send(ref, ref, *ici(j, 15 + a), ups[orders[j][2]])
            share(j, ref, chunk_group(a, 3))
            ref = third[j](step(c3[j], 1), q)
            arrived(ref, *ici(j, 11 + a), me)
            if a in (1, 3):
                send(ref, ref, *ici(j, 15 + a), downs[orders[j][2]])
            share(j, ref, chunk_group(a, 1))

    def far_arrival(a):
        for j in range(3):
            ref = third[j](step(c3[j], 2), step(c2[j], a))
            arrived(ref, *ici(j, 15 + a), me)
            share(j, ref, chunk_group(a, 2))

    for j in range(3):
        ref = first[j](c1[j])
        send(ref, ref, *ici(j, 0), ups[orders[j][0]])
        send(ref, ref, *ici(j, 0), downs[orders[j][0]])
        send(ref, ref, *ici(j, 0), fars[orders[j][0]])
    pltpu.make_async_copy(win, win, loc.at[1]).wait()
    for j in range(3):
        arrived(pot.at[j, pl.ds(0, 3), 0, pl.ds(0, 128)], *ici(j, 0), me)
        ref = second[j](c2[j])
        send(ref, ref, *ici(j, 3), ups[orders[j][1]])
        send(ref, ref, *ici(j, 4), downs[orders[j][1]])
        third_send(j, 0)
        share(j, ref, 0)
    for j in range(3):
        ref = second[j](step(c2[j], 3))
        arrived(ref, *ici(j, 3), me)
        half = second[j](step(c2[j], 3), 0)
        send(half, half, *ici(j, 5), ups[orders[j][1]])
        third_send(j, 3)
        share(j, ref, 0)
        ref = second[j](step(c2[j], 1))
        arrived(ref, *ici(j, 4), me)
        half = second[j](step(c2[j], 1), 1)
        send(half, half, *ici(j, 6), downs[orders[j][1]])
        third_send(j, 1)
        share(j, ref, 0)
    third_arrival(0)
    for j in range(3):
        far = step(c2[j], 2)
        arrived(second[j](far, 0), *ici(j, 5), me)
        arrived(second[j](far, 1), *ici(j, 6), me)
        third_send(j, 2)
        share(j, second[j](far), 0)

    started = [False]

    def add(points, row_starts, size, last=False):
        lhs = jnp.concatenate([
            jnp.concatenate([pot[j, yy, xx, pl.ds(pl.multiple_of(s, 128), size), :] for s in row_starts], axis=0)
            for j, yy, xx in points], axis=1)
        rhs = jnp.concatenate([win[(yy * 4 + xx) * 3 + j] for j, yy, xx in points], axis=1)
        value = lax.dot_general(lhs, rhs, (((1,), (1,)), ((), ())), preferred_element_type=F32)
        if not started[0]:
            acc[...] = value
            started[0] = True
            return
        if last:
            value = (value + acc[...]).astype(BF)
            for kk in range(2):
                for zz in range(4):
                    for i in range(8):
                        here, there = kk * 512 + zz * 128 + i * 16, (kk * 8 + i) * 64 + zz * 16
                        out_ref[there:there + 16] = value[here:here + 16]
            return
        for i, s in enumerate(row_starts):
            where = pl.ds(pl.multiple_of(s, 128), size)
            acc[where, :] += value[i * size:(i + 1) * size]

    def both(s):
        return [s * 128, 512 + s * 128]

    def add_second(j):
        shared(j, 0, pot.at[j, :, 0, pl.ds(0, 512)])
        if j == 0:
            add([(0, q, x) for q in range(4)], [0], 1024)
        if j == 1:
            add([(1, y, q) for q in range(4)], [0], 1024)
        if j == 2:
            add([(2, a, b) for a in range(4) for b in range(4)], both(z), 128)

    def add_third(j, chunk_pair, others, last=False):
        shared(j, chunk_group(chunk_pair[0], others[0]), pot.at[j, pl.ds(0, 2 * len(others)), 0, pl.ds(0, 512)])
        qs = [step(c2[j], a) for a in chunk_pair]
        ss = [step(c3[j], b) for b in others]
        if j == 0:
            add([(0, q, s) for q in qs for s in ss], [0], 1024, last)
        if j == 1:
            add([(1, s, b) for s in ss for b in range(4)], both(qs[0]) + both(qs[1]), 128)
        if j == 2:
            add([(2, a, q) for a in range(4) for q in qs], [v for s in ss for v in both(s)], 128)

    third_arrival(3)
    add_second(0)
    add_second(1)
    third_arrival(1)
    add_second(2)
    add_third(0, (0, 3), (3, 1))
    third_arrival(2)
    add_third(1, (0, 3), (3, 1))
    add_third(2, (0, 3), (3, 1))
    far_arrival(0)
    for j in range(3):
        add_third(j, (1, 2), (3, 1))
    far_arrival(3)
    far_arrival(1)
    far_arrival(2)
    for j in range(3):
        add_third(j, (0, 3), (2,))
    for j in (1, 2, 0):
        add_third(j, (1, 2), (2,), j == 0)
    left(halves.at[1 - k], half_s.at[0], me)
    left(pot.at[:, :, :, half_rows()], d2d_s.at[0], me)
    left(pot.at[:, pl.ds(0, 3), pl.ds(0, 3), pl.ds(0, 896)], ici_s.at[0], me)


def mask_kernel(least, coupling, out_ref):
    shape = out_ref.shape
    ahead = lax.broadcasted_iota(jnp.int32, shape, 1) - lax.broadcasted_iota(jnp.int32, shape, 0)
    value = coupling[...].astype(F32)
    keep = ahead >= least[0] + pl.program_id(0) * shape[0]
    out_ref[...] = jnp.where(keep, value, jnp.zeros_like(value)).astype(BF)


def sems(*shape):
    return pltpu.SemaphoreType.DMA(shape)


ANY = pl.BlockSpec(memory_space=pl.ANY)
VMEM = pl.BlockSpec(memory_space=pltpu.VMEM)


def shards(
    occ_coef, vir_coef, atom_counts, occ_index, vir_index, interaction, window_charges, panel_start
):
    coupling = pl.pallas_call(
        panel_kernel,
        out_shape=jax.ShapeDtypeStruct((1024, 1024), BF),
        in_specs=[ANY] * 7,
        out_specs=VMEM,
        scratch_shapes=[
            pltpu.VMEM((1, 64), jnp.int32),
            pltpu.VMEM((1, 64), jnp.int32),
            pltpu.VMEM((1, 768), jnp.int32),
            pltpu.VMEM((8, 128), jnp.int32),
            pltpu.VMEM((16, 8, 128), jnp.int32),
            pltpu.VMEM((16, 64, 128), BF),
            pltpu.VMEM((16, 128, 128), BF),
            pltpu.VMEM((1024, 1024), BF),
            pltpu.VMEM((1024, 2048), BF),
            pltpu.VMEM((1024, 128), F32),
            pltpu.VMEM((1024, 128), F32),
            pltpu.VMEM((2048, 768), BF),
            pltpu.VMEM((16, 64, 128), BF),
            pltpu.VMEM((16, 64, 128), BF),
            pltpu.VMEM((4, 16, 768), BF),
            pltpu.VMEM((4, 4, 4, 16, 768), BF),
            pltpu.VMEM((4, 768, 384), BF),
            pltpu.VMEM((2, 128, 384), F32),
            pltpu.VMEM((128, 384), F32),
            pltpu.VMEM((3, 4, 4, 1024, 128), BF),
            pltpu.VMEM((48, 1024, 128), BF),
            pltpu.VMEM((1024, 1024), F32),
            sems(1), sems(1), sems(1), sems(1), sems(1), sems(4), sems(1), sems(1),
            sems(1), sems(4), sems(1), sems(1), sems(1), sems(2, 12), sems(1), sems(1),
            sems(1), sems(3, 19), sems(1), sems(3, 5), sems(5),
        ],
        compiler_params=pltpu.CompilerParams(
            collective_id=0, has_side_effects=True, vmem_limit_bytes=60 * 2**20
        ),
    )(occ_index[None], vir_index[None], occ_coef, vir_coef, atom_counts, interaction, window_charges)
    least = panel_start - lax.axis_index(("row", "col")) * window_charges.shape[0]
    return pl.pallas_call(
        mask_kernel,
        grid=(2,),
        out_shape=jax.ShapeDtypeStruct((1024, 1024), BF),
        in_specs=[pl.BlockSpec(memory_space=pltpu.SMEM), pl.BlockSpec((512, 1024), lambda i: (i, 0))],
        out_specs=pl.BlockSpec((512, 1024), lambda i: (i, 0)),
    )(least, coupling)


def solution(mesh):
    placed = (
        P("row", "col"),
        P("row", "col"),
        P("col", None),
        P("row"),
        P("row"),
        P("col", "row"),
        P(("row", "col"), None),
        P(),
    )
    return jax.shard_map(
        shards, mesh=mesh, in_specs=placed, out_specs=P(None, ("row", "col")), check_vma=False
    )
```

time: 94.2 us -> 90.4 us (0.960)
  other arithmetic: 3.46 us -> 0 us
    select_n x1 -> x0, other arithmetic: 3.46 us -> none  [shards(): return jnp.where(upper_mask, coupling, jnp.zeros_like(coupling))]
    pallas_call x1, Pallas kernels: 89.9 us -> 86.7 us  [shards(): pl.pallas_call(panel_kernel, out_shape=jax.ShapeDtypeStruct((1024, 1024),...]
    pallas_call x0 -> x1, Pallas kernels: none -> 2.87 us  [shards(): pl.pallas_call(mask_kernel, grid=(2,), out_shape=jax.ShapeDtypeStruct((10...]
where the time goes in v3:
time: 90.4 us; the launch traced here: 90.2 us
  Pallas kernels  89.6 us (99%)
    pallas_call x1, Pallas kernels, shards(): pl.pallas_call(panel_kernel, out_shape=jax.ShapeDtypeStruct((1024, 1024),...  86.7 us
    pallas_call x1, Pallas kernels, shards(): pl.pallas_call(mask_kernel, grid=(2,), out_shape=jax.ShapeDtypeStruct((10...  2.87 us

profile of v3, /device:TPU:1, one launch (start us, length us, event | category | flops | bytes accessed | tf_op | source)
XLA Modules:
  0.0 90.2 jit_solution(17376666171532086635)
XLA Ops:
  0.7 86.7 %shard_map.82.coupling = bf16[1024,1024]{1,0:T(8,128)(2,1)} custom-call(s32[1,64]{1,0:T(1,128)} %bitcast.3, s32[1,64]{1,0:T(1,128)} %bitcast.4, bf16[64,2048]{1,0:T(8,128)(2,1)} %occ_hbm.1, bf16[128,2048]{1,0:T(8,128)(2,1)} %vir_hbm.1, s32[1,768]{1,0:T(1,128)} %counts_hbm.1, bf16[768,384]{1,0:T(8,128)(2,1)} %inter_hbm.1, bf16[1024,6144]{1,0:T(8,128)(2,1)} %win_hbm.1), custom_call_target="tpu_custom_call" | custom-call | tf_op jit(solution)/shard_map/pallas_call | solution.py:427
  87.4 2.9 %shard_map.83 = bf16[1024,1024]{1,0:T(8,128)(2,1)} custom-call(s32[1]{0:T(128)S(6)} %sub.7.least, bf16[1024,1024]{1,0:T(8,128)(2,1)} %shard_map.82.coupling), custom_call_target="tpu_custom_call" | custom-call | tf_op jit(solution)/shard_map/pallas_call | solution.py:464

commit v4 on v3

--- a/solution.py
+++ b/solution.py
@@ -55,7 +55,11 @@
     me = device(y, x, z, k)
     r = y * 4 + x
     twin = device(y, x, z, 1 - k)
-    plane = [(step(y, dy), step(x, dx)) for dy in (0, 1, 3, 2) for dx in range(4) if dy or dx]
+    hops = (
+        (0, 1), (1, 0), (0, 3), (3, 0), (1, 1), (3, 3), (1, 3), (3, 1),
+        (0, 2), (2, 0), (1, 2), (2, 1), (3, 2), (2, 3), (2, 2),
+    )
+    plane = [(step(y, dy), step(x, dx)) for dy, dx in hops]
     small = [
         pltpu.make_async_copy(occ_index, occ_own, loc.at[2]),
         pltpu.make_async_copy(vir_index, vir_own, loc.at[3]),
@@ -390,14 +394,16 @@
     third_arrival(2)
     add_third(1, (0, 3), (3, 1))
     add_third(2, (0, 3), (3, 1))
+    add_third(0, (1, 2), (3, 1))
     far_arrival(0)
-    for j in range(3):
-        add_third(j, (1, 2), (3, 1))
+    add_third(1, (1, 2), (3, 1))
     far_arrival(3)
+    add_third(2, (1, 2), (3, 1))
     far_arrival(1)
+    add_third(0, (0, 3), (2,))
     far_arrival(2)
-    for j in range(3):
-        add_third(j, (0, 3), (2,))
+    add_third(1, (0, 3), (2,))
+    add_third(2, (0, 3), (2,))
     for j in (1, 2, 0):
         add_third(j, (1, 2), (2,), j == 0)
     left(halves.at[1 - k], half_s.at[0], me)

time: 90.4 us -> 88.9 us (0.983)
  Pallas kernels: 89.6 us -> 88.1 us
    pallas_call x1, Pallas kernels: 86.7 us -> 85.2 us  [shards(): pl.pallas_call(panel_kernel, out_shape=jax.ShapeDtypeStruct((1024, 1024),...]
where the time goes in v4:
time: 88.9 us; the launch traced here: 88.8 us
  Pallas kernels  88.1 us (99%)
    pallas_call x1, Pallas kernels, shards(): pl.pallas_call(panel_kernel, out_shape=jax.ShapeDtypeStruct((1024, 1024),...  85.2 us
    pallas_call x1, Pallas kernels, shards(): pl.pallas_call(mask_kernel, grid=(2,), out_shape=jax.ShapeDtypeStruct((10...  2.87 us

profile of v4, /device:TPU:1, one launch (start us, length us, event | category | flops | bytes accessed | tf_op | source)
XLA Modules:
  0.0 88.8 jit_solution(16693765137723307566)
XLA Ops:
  0.7 85.2 %shard_map.82.coupling = bf16[1024,1024]{1,0:T(8,128)(2,1)} custom-call(s32[1,64]{1,0:T(1,128)} %bitcast.3, s32[1,64]{1,0:T(1,128)} %bitcast.4, bf16[64,2048]{1,0:T(8,128)(2,1)} %occ_hbm.1, bf16[128,2048]{1,0:T(8,128)(2,1)} %vir_hbm.1, s32[1,768]{1,0:T(1,128)} %counts_hbm.1, bf16[768,384]{1,0:T(8,128)(2,1)} %inter_hbm.1, bf16[1024,6144]{1,0:T(8,128)(2,1)} %win_hbm.1), custom_call_target="tpu_custom_call" | custom-call | tf_op jit(solution)/shard_map/pallas_call | solution.py:433
  85.9 2.9 %shard_map.83 = bf16[1024,1024]{1,0:T(8,128)(2,1)} custom-call(s32[1]{0:T(128)S(6)} %sub.7.least, bf16[1024,1024]{1,0:T(8,128)(2,1)} %shard_map.82.coupling), custom_call_target="tpu_custom_call" | custom-call | tf_op jit(solution)/shard_map/pallas_call | solution.py:470
